TPU v7x, 32 devices: a whole 2x2x4 slice. The times are simulated.
32 devices in a mesh: groups: 2 (over y), ctx: 16 (over z, x, core).
Axes of the slice: x: 2, y: 2, z: 4, core: 2. Of those that a mesh axis runs over, the one named last changes fastest.
Arguments:
- queries: bfloat16 [3072, 2048], P(('groups', 'ctx')), parts along dimension 0
- new_keys: bfloat16 [3072, 512], P(('groups', 'ctx')), parts along dimension 0
- new_values: bfloat16 [3072, 512], P(('groups', 'ctx')), parts along dimension 0, may hold values from -6 to 6
- prefix_keys: bfloat16 [512, 512], P(('groups', 'ctx')), parts along dimension 0, may hold values from -6 to 6
- prefix_values: bfloat16 [512, 512], P(('groups', 'ctx')), parts along dimension 0, may hold values from -6 to 6
- prefix_len: int32 [32], P(('groups', 'ctx')), parts along dimension 0, may hold values from 8 to 16, as said below
- owners: int32 [192], P(('groups', 'ctx')), parts along dimension 0, may hold values from 0 to 15, as said below
Outputs:
- attended: bfloat16 [3072, 2048], P(('groups', 'ctx')), parts along dimension 0
- log_mass: float32 [32, 1536], P('groups', 'ctx'), parts along dimension 0
- owned_cache: bfloat16 [384, 16, 1024], P(('groups', 'ctx')), parts along dimension 0
There are 2 independent parts, one for each index of `groups`. A program takes and returns all parts, laid end to end along the dimension named above; each array names one. Nothing has to cross between parts.
Inputs may be any that keep to these rules, and one draw needn't show every extreme that they name: `prefix_len`: slots of a shard from its count on are stale; some shard has all 16 slots live. `owners`: each device owns at most 12 fresh blocks, and some device owns exactly 12.
All inputs are finite; a program needn't handle non-finite values.
Results may differ from a plain program's by a relative error of at most 0.0049.
Values may be sent and summed in bfloat16 or wider, within the bound.
A program may use at most 128 MiB of HBM per device.

v0:
```python
import jax
import jax.numpy as jnp
from jax import lax
from jax.sharding import PartitionSpec as P

H = 16
G = 4
DH = 128
Q_DEV = 96
P_DEV = 16
BLK = 16
CAP = 12


def block_size(total_rows):
    return max((size for size in range(1, 1537) if total_rows % size == 0))


def per_device(queries, new_keys, new_values, prefix_keys, prefix_values, prefix_len, owners):
    per_group = H // G
    device_rank = lax.axis_index("ctx")
    cycle_size = lax.axis_size("ctx")
    all_owners, all_live = (
        lax.all_gather(owners, "ctx", axis=0, tiled=True),
        lax.all_gather(prefix_len, "ctx", axis=0, tiled=True),
    )
    block_count = all_owners.shape[0]
    same_owner = all_owners[:, None] == all_owners[None, :]
    lower = jnp.arange(block_count)[None, :] < jnp.arange(block_count)[:, None]
    ranks = jnp.sum((same_owner & lower).astype(jnp.int32), axis=1)
    match = (all_owners[None, :] == device_rank) & (ranks[None, :] == jnp.arange(CAP)[:, None])
    present = jnp.any(match, axis=1)
    wanted = jnp.sum(jnp.where(match, jnp.arange(block_count)[None, :], 0), axis=1)
    want_token = (wanted[:, None] * BLK + jnp.arange(BLK)[None, :]).reshape(-1)
    row_present = jnp.repeat(present, BLK)
    query_heads = queries.reshape(Q_DEV, G, per_group, DH)
    my_tokens = device_rank * Q_DEV + jnp.arange(Q_DEV)
    scale = DH ** (-0.5)

    def attend_rows(state, piece, global_start, pre_width, fresh_width):
        count_rows = piece.shape[0]
        row_index = global_start + jnp.arange(count_rows)
        width = pre_width + fresh_width
        shard_id = row_index // width
        offset = row_index % width
        is_prefix = offset < pre_width
        live_here = jnp.take(all_live, jnp.clip(shard_id, 0, cycle_size - 1))
        token_pos = shard_id * Q_DEV + offset - pre_width
        visible = jnp.where(
            is_prefix[None, :],
            (offset < live_here)[None, :],
            token_pos[None, :] <= my_tokens[:, None],
        )
        running, totals, accum = state
        keys_part = piece[:, : G * DH].reshape(count_rows, G, DH)
        values_part = piece[:, G * DH :].reshape(count_rows, G, DH)
        scores = (
            jnp.einsum("qgjd,kgd->gjqk", query_heads, keys_part, preferred_element_type=jnp.float32)
            * scale
        )
        scores = jnp.where(visible[None, None], scores, -1e30)
        new_top = jnp.maximum(running, jnp.max(scores, axis=-1))
        weights = jnp.where(visible[None, None], jnp.exp(scores - new_top[..., None]), 0.0)
        factor = jnp.exp(running - new_top)
        totals = totals * factor + jnp.sum(weights, axis=-1)
        accum = accum * factor[..., None] + jnp.einsum(
            "gjqk,kgd->gjqd",
            weights.astype(jnp.bfloat16),
            values_part,
            preferred_element_type=jnp.float32,
        )
        return (new_top, totals, accum)

    def fold_piece(state, piece, start, pre_width, fresh_width):
        count_rows = piece.shape[0]
        step_rows = block_size(count_rows)
        steps_count = count_rows // step_rows
        if steps_count == 1:
            return attend_rows(state, piece, start, pre_width, fresh_width)
        pieces = piece.reshape(steps_count, step_rows, piece.shape[1])

        def advance(carried, inputs):
            block_rows, block_id = inputs
            return (
                attend_rows(
                    carried, block_rows, start + block_id * step_rows, pre_width, fresh_width
                ),
                None,
            )

        state, unused = lax.scan(advance, state, (pieces, jnp.arange(steps_count)))
        return state

    start_state = (
        jnp.full((G, per_group, Q_DEV), -1e30, jnp.float32),
        jnp.zeros((G, per_group, Q_DEV), jnp.float32),
        jnp.zeros((G, per_group, Q_DEV, DH), jnp.float32),
    )
    owned_start = jnp.zeros((CAP * BLK, 2 * G * DH), jnp.bfloat16)
    prefix_rows = jnp.concatenate([prefix_keys, prefix_values], 1)
    fresh_rows = jnp.concatenate([new_keys, new_values], 1)
    stacked = jnp.concatenate([prefix_rows, fresh_rows], 0)
    carried = (start_state, owned_start)
    piece = lax.all_gather(stacked, "ctx", axis=0, tiled=True)
    state = fold_piece(carried[0], piece, jnp.int32(0), P_DEV, Q_DEV)
    count_rows = piece.shape[0]
    width = P_DEV + Q_DEV
    target = want_token // Q_DEV * width + P_DEV + want_token % Q_DEV
    inside = (target >= 0) & (target < count_rows) & row_present
    taken = jnp.take(piece, jnp.clip(target, 0, count_rows - 1), axis=0)
    owned = jnp.where(inside[:, None], taken, carried[1])
    running, totals, accum = state
    attended = (
        (accum / totals[..., None])
        .transpose(2, 0, 1, 3)
        .reshape(Q_DEV, H * DH)
        .astype(jnp.bfloat16)
    )
    log_mass = (running + jnp.log(totals)).reshape(H, Q_DEV)
    owned_cache = owned.reshape(CAP, BLK, 2 * G * DH)
    return (attended, log_mass, owned_cache)


def solution(mesh):
    return jax.shard_map(
        per_device,
        mesh=mesh,
        in_specs=(
            P(("groups", "ctx"), None),
            P(("groups", "ctx"), None),
            P(("groups", "ctx"), None),
            P(("groups", "ctx"), None),
            P(("groups", "ctx"), None),
            P(("groups", "ctx")),
            P(("groups", "ctx")),
        ),
        out_specs=(
            P(("groups", "ctx"), None),
            P("groups", "ctx"),
            P(("groups", "ctx"), None, None),
        ),
        check_vma=False,
    )
```

profile of v0, /device:TPU:0, one launch (start us, length us, event | category | flops | bytes accessed | tf_op | source)
XLA Modules:
  0.0 134.4 jit_solution(13546602472778991433)
XLA Ops:
  7.2 1.7 %maximum_maximum_fusion = bf16[112,1024]{1,0:T(8,128)(2,1)} fusion(bf16[96,512]{1,0:T(8,128)(2,1)} %param.11, bf16[96,512]{1,0:T(8,128)(2,1)} %param.10, bf16[16,512]{1,0:T(8,128)(2,1)} %param.13, bf16[16,512]{1,0:T(8,128)(2,1)} %param.12), kind=kLoop, calls=%fused_computation.56 | loop fusion | flops 917504 | bytes 458752 | tf_op jit(solution)/shard_map/concatenate | solution.py:102
  9.5 1.2 dynamic-slice
  13.0 13.8 %all-reduce.2 = (s32[16]{0:T(128)S(1)}, s32[96]{0:T(128)S(1)}) all-reduce(s32[16]{0:T(128)S(1)} %dynamic-update-slice, s32[96]{0:T(128)S(1)} %dynamic-update-slice.1), channel_id=1, replica_groups=mesh['groups'=2,'ctx'=16] {'ctx'}, use_global_device_ids=true, to_apply=%add | all-reduce | flops 112 | bytes 896
  26.9 1.3 reshape.304
  29.1 32.1 %all-gather.2.cloned.1.call-done = bf16[1792,1024]{1,0:T(8,128)(2,1)} async-done(((bf16[112,1024]{1,0:T(8,128)(2,1)}), bf16[1792,1024]{1,0:T(8,128)(2,1)}) %all-gather.2.cloned.1.call-update) | async-done | bytes 3670032 | tf_op jit(solution)/shard_map/all_gather | solution.py:104
  61.3 58.3 %while.17 = (s32[]{:T(128)}, f32[4,4,96]{2,1,0:T(4,128)S(1)}, f32[4,4,96]{2,1,0:T(4,128)S(1)}, f32[4,4,96,128]{3,2,1,0:T(8,128)}, s32[2]{0:T(128)S(1)}, /*index=...) while((s32[]{:T(128)}, f32[4,4,96]{2,1,0:T(4,128)S(1)}, ...), condition=%wide.region_3.4_spmd.clone, body=%wide.region_0.3_spmd.clone.sunk | while | flops 723442048 | bytes 60115420 | solution.py:91
  63.6 4.5 %fusion.59 = s32[896]{0:T(1024)S(1)} fusion(s32[]{:T(128)} %bitcast.88, s32[]{:T(128)} %bitcast.89, s32[]{:T(128)} %bitcast.90, s32[]{:T(128)} %bitcast.91, s32[]{:T(128)} %bitcast.92, s32[]{:T(128)} %bitcast.93, s32[]{:T(128)} %bitcast.94, s32[]{:T(128)} %bitcast.87), kind=kLoop, calls=%fused_computation.47.clone.1 | loop fusion | flops 22400 | bytes 3616 | tf_op jit(solution)/shard_map/while/body/eval_jaxpr/jit(_take)/gather | solution.py:47
  68.1 5.5 %fusion.60 = pred[896]{0:T(1024)(128)(4,1)S(1)} fusion(pred[896]{0:T(1024)(128)(4,1)S(1)} %get-tuple-element.316, pred[896]{0:T(1024)(128)(4,1)S(1)} %get-tuple-element.317, pred[896]{0:T(1024)(128)(4,1)S(1)} %get-tuple-element.318, pred[896]{0:T(1024)(128)(4,1)S(1)} %get-tuple-element.319, pred[896]{0:T(1024)(128)(4,1)S(1)} %get-tuple-element.320, ...), kind=kLoop, calls=%fused_computation.37.clone.1 | loop fusion | flops 27776 | bytes 12584 | tf_op jit(solution)/shard_map/while/body/eval_jaxpr/lt | solution.py:51
  73.7 2.9 %constant_dynamic-slice_fusion.2 = bf16[1,896,1024]{2,1,0:T(8,128)(2,1)} fusion(bf16[2,896,1024]{2,1,0:T(8,128)(2,1)} %get-tuple-element.376, s32[]{:T(128)S(6)} %copy.36), kind=kLoop, calls=%fused_computation.49.clone.1 | loop fusion | bytes 3670020 | tf_op jit(solution)/shard_map/while/body/jit(dynamic_index_in_dim)/dynamic_slice | solution.py:91
  76.6 3.1 %copy.29 = bf16[1,896,1024]{1,2,0:T(8,128)(2,1)S(1)} copy(bf16[1,896,1024]{2,1,0:T(8,128)(2,1)} %constant_dynamic-slice_fusion.2) | data formatting | bytes 3670016 | tf_op jit(solution)/shard_map/while/body/jit(dynamic_index_in_dim)/dynamic_slice | solution.py:91
  79.9 3.5 %fusion.63 = (f32[4,4,96]{2,1,0:T(4,128)S(1)}, f32[4,896,96,4]{1,2,3,0:T(8,128)}) fusion(pred[96,896]{1,0:T(8,128)(4,1)S(1)} %compare_select_fusion.12, bf16[896,4,128,1]{0,2,3,1:T(8,128)(2,1)S(1)} %bitcast.108, bf16[96,4,4,128]{3,0,2,1:T(8,128)(2,1)S(1)} %get-tuple-element.377), kind=kOutput, calls=%fused_computation.4.clone.1 | convolution fusion | flops 356448768 | bytes 6907904 | tf_op jit(solution)/shard_map/while/body/eval_jaxpr/qgjd,kgd->gjqk/dot_general | solution.py:58
  83.4 4.4 %fusion.64 = f32[4,4,96]{2,1,0:T(4,128)S(1)} fusion(f32[4,896,96,4]{1,2,3,0:T(8,128)} %get-tuple-element.342, f32[4,4,96]{2,1,0:T(4,128)S(1)} %select_maximum_fusion.2, pred[96,896]{1,0:T(8,128)(4,1)S(1)} %compare_select_fusion.12), kind=kLoop, calls=%fused_computation.6.clone.1 | loop fusion | flops 6879744 | bytes 5603328 | tf_op jit(solution)/shard_map/while/body/eval_jaxpr/reduce_sum | solution.py:65
  87.8 1.7 %fusion.66 = f32[4,4,96,128]{3,2,1,0:T(8,128)S(1)} fusion(bf16[896,4,128,1]{0,2,3,1:T(8,128)(2,1)S(1)} %bitcast.111, f32[4,896,96,4]{1,2,3,0:T(8,128)S(1)} %copy-done, f32[4,4,96]{2,1,0:T(4,128)S(1)} %select_maximum_fusion.2, pred[96,896]{1,0:T(8,128)(4,1)S(1)} %compare_select_fusion.12, f32[4,4,96,128]{3,2,1,0:T(8,128)S(1)} %copy-done.1, ...), kind=kOutput, calls=%fused_computation.9.clone.1 | convolution fusion | flops 359792640 | bytes 8093697 | tf_op jit(solution)/shard_map/while/body/eval_jaxpr/gjqk,kgd->gjqd/dot_general | solution.py:66
  89.5 0.9 copy-done.2
  92.7 4.5 %fusion.59 = s32[896]{0:T(1024)S(1)} fusion(s32[]{:T(128)} %bitcast.88, s32[]{:T(128)} %bitcast.89, s32[]{:T(128)} %bitcast.90, s32[]{:T(128)} %bitcast.91, s32[]{:T(128)} %bitcast.92, s32[]{:T(128)} %bitcast.93, s32[]{:T(128)} %bitcast.94, s32[]{:T(128)} %bitcast.87), kind=kLoop, calls=%fused_computation.47.clone.1 | loop fusion | flops 22400 | bytes 3616 | tf_op jit(solution)/shard_map/while/body/eval_jaxpr/jit(_take)/gather | solution.py:47
  97.2 5.5 %fusion.60 = pred[896]{0:T(1024)(128)(4,1)S(1)} fusion(pred[896]{0:T(1024)(128)(4,1)S(1)} %get-tuple-element.316, pred[896]{0:T(1024)(128)(4,1)S(1)} %get-tuple-element.317, pred[896]{0:T(1024)(128)(4,1)S(1)} %get-tuple-element.318, pred[896]{0:T(1024)(128)(4,1)S(1)} %get-tuple-element.319, pred[896]{0:T(1024)(128)(4,1)S(1)} %get-tuple-element.320, ...), kind=kLoop, calls=%fused_computation.37.clone.1 | loop fusion | flops 27776 | bytes 12584 | tf_op jit(solution)/shard_map/while/body/eval_jaxpr/lt | solution.py:51
  102.9 2.9 %constant_dynamic-slice_fusion.2 = bf16[1,896,1024]{2,1,0:T(8,128)(2,1)} fusion(bf16[2,896,1024]{2,1,0:T(8,128)(2,1)} %get-tuple-element.376, s32[]{:T(128)S(6)} %copy.36), kind=kLoop, calls=%fused_computation.49.clone.1 | loop fusion | bytes 3670020 | tf_op jit(solution)/shard_map/while/body/jit(dynamic_index_in_dim)/dynamic_slice | solution.py:91
  105.8 3.1 %copy.29 = bf16[1,896,1024]{1,2,0:T(8,128)(2,1)S(1)} copy(bf16[1,896,1024]{2,1,0:T(8,128)(2,1)} %constant_dynamic-slice_fusion.2) | data formatting | bytes 3670016 | tf_op jit(solution)/shard_map/while/body/jit(dynamic_index_in_dim)/dynamic_slice | solution.py:91
  109.0 3.5 %fusion.63 = (f32[4,4,96]{2,1,0:T(4,128)S(1)}, f32[4,896,96,4]{1,2,3,0:T(8,128)}) fusion(pred[96,896]{1,0:T(8,128)(4,1)S(1)} %compare_select_fusion.12, bf16[896,4,128,1]{0,2,3,1:T(8,128)(2,1)S(1)} %bitcast.108, bf16[96,4,4,128]{3,0,2,1:T(8,128)(2,1)S(1)} %get-tuple-element.377), kind=kOutput, calls=%fused_computation.4.clone.1 | convolution fusion | flops 356448768 | bytes 6907904 | tf_op jit(solution)/shard_map/while/body/eval_jaxpr/qgjd,kgd->gjqk/dot_general | solution.py:58
  112.5 4.4 %fusion.64 = f32[4,4,96]{2,1,0:T(4,128)S(1)} fusion(f32[4,896,96,4]{1,2,3,0:T(8,128)} %get-tuple-element.342, f32[4,4,96]{2,1,0:T(4,128)S(1)} %select_maximum_fusion.2, pred[96,896]{1,0:T(8,128)(4,1)S(1)} %compare_select_fusion.12), kind=kLoop, calls=%fused_computation.6.clone.1 | loop fusion | flops 6879744 | bytes 5603328 | tf_op jit(solution)/shard_map/while/body/eval_jaxpr/reduce_sum | solution.py:65
  117.0 1.7 %fusion.66 = f32[4,4,96,128]{3,2,1,0:T(8,128)S(1)} fusion(bf16[896,4,128,1]{0,2,3,1:T(8,128)(2,1)S(1)} %bitcast.111, f32[4,896,96,4]{1,2,3,0:T(8,128)S(1)} %copy-done, f32[4,4,96]{2,1,0:T(4,128)S(1)} %select_maximum_fusion.2, pred[96,896]{1,0:T(8,128)(4,1)S(1)} %compare_select_fusion.12, f32[4,4,96,128]{3,2,1,0:T(8,128)S(1)} %copy-done.1, ...), kind=kOutput, calls=%fused_computation.9.clone.1 | convolution fusion | flops 359792640 | bytes 8093697 | tf_op jit(solution)/shard_map/while/body/eval_jaxpr/gjqk,kgd->gjqd/dot_general | solution.py:66
  119.6 1.4 %fusion.23 = bf16[96,4,4,128]{3,0,2,1:T(8,128)(2,1)S(1)} fusion(f32[4,4,96,128]{3,2,1,0:T(8,128)} %get-tuple-element.122, f32[4,4,96]{2,1,0:T(4,128)S(1)} %get-tuple-element.123), kind=kLoop, calls=%fused_computation.55 | loop fusion | flops 393216 | bytes 1185792 | tf_op jit(solution)/shard_map/convert_element_type | solution.py:117
  121.2 1.0 convert_element_type.20
  122.8 3.8 %gather_fusion = bf16[192,1024]{1,0:T(8,128)(2,1)S(1)} fusion(bf16[1792,1024]{1,0:T(8,128)(2,1)} %bitcast.110, s32[1024]{0:T(1024)S(1)} %pad_clamp_fusion), kind=kCustom, calls=%fused_computation | custom fusion | bytes 787200 | tf_op jit(solution)/shard_map/jit(_take)/gather | solution.py:110
  (67 shorter events, 9.1 us)
Async XLA Ops:
  7.2 54.1 %all-gather.2.cloned.1.call-start = ((), (), s32[]{:S(2)}) async-start(), calls=%async_computation | async-start | bytes 3899392 | tf_op jit(solution)/shard_map/all_gather | solution.py:104
  79.9 8.0 %copy-start.1 = (f32[4,4,96,128]{3,2,1,0:T(8,128)S(1)}, f32[4,4,96,128]{3,2,1,0:T(8,128)}, u32[]{:S(2)}) copy-start(f32[4,4,96,128]{3,2,1,0:T(8,128)} %get-tuple-element.361) | copy-start | bytes 2359300 | tf_op jit(solution)/shard_map/while
  83.4 4.5 %copy-start = (f32[4,896,96,4]{1,2,3,0:T(8,128)S(1)}, f32[4,896,96,4]{1,2,3,0:T(8,128)}, u32[]{:S(2)}) copy-start(f32[4,896,96,4]{1,2,3,0:T(8,128)} %get-tuple-element.342) | copy-start | bytes 16515076 | tf_op jit(solution)/shard_map/while
  89.5 0.9 copy-start.2
  109.0 8.0 %copy-start.1 = (f32[4,4,96,128]{3,2,1,0:T(8,128)S(1)}, f32[4,4,96,128]{3,2,1,0:T(8,128)}, u32[]{:S(2)}) copy-start(f32[4,4,96,128]{3,2,1,0:T(8,128)} %get-tuple-element.361) | copy-start | bytes 2359300 | tf_op jit(solution)/shard_map/while
  112.5 4.5 %copy-start = (f32[4,896,96,4]{1,2,3,0:T(8,128)S(1)}, f32[4,896,96,4]{1,2,3,0:T(8,128)}, u32[]{:S(2)}) copy-start(f32[4,896,96,4]{1,2,3,0:T(8,128)} %get-tuple-element.342) | copy-start | bytes 16515076 | tf_op jit(solution)/shard_map/while
  118.7 0.9 copy-start.2
Sparse Core Ops, SparseCore 0:
  10.9 50.3 all-gather.1
where the time goes:
time: 135 us; the launch traced here: 134 us
  other arithmetic  35 us (26%)
  waiting for transfers between devices  32.1 us (24%)
  local copies, waits for them, and re-layouts  26.1 us (19%)
  between operations  15.4 us (11%)
  blocking collectives  13.8 us (10%)
  matrix products  10.4 us (8%)
  loops' own time  1.54 us (1%)
    all_gather x1, waiting for transfers between devices, per_device(): piece = lax.all_gather(stacked, 'ctx', axis=0, tiled=True)  32.1 us
    unnamed x1, blocking collectives  13.8 us
    dynamic_slice x6, local copies, waits for them, and re-layouts, fold_piece(): state, unused = lax.scan(advance, state, (pieces, jnp.arange(steps_count)))  13.1 us
    lt x2, other arithmetic, attend_rows(): offset < live_here  11 us
    gather x12, other arithmetic, attend_rows(): live_here = jnp.take(all_live, jnp.clip(shard_id, 0, cycle_size - 1))  9.61 us
    reduce_sum x2, other arithmetic, attend_rows(): totals = totals * factor + jnp.sum(weights, axis=-1)  8.81 us
    dot_general x2, matrix products, attend_rows(): jnp.einsum('qgjd,kgd->gjqk', query_heads, keys_part, preferred_element_ty...  7.01 us
    gather x1, local copies, waits for them, and re-layouts, per_device(): taken = jnp.take(piece, jnp.clip(target, 0, count_rows - 1), axis=0)  3.81 us
  transfers between devices with their start and end apart: 1, of which 1 were waited for; matrix products, arithmetic and copies ran while one was open for 4% of the time, Pallas kernels for 0%

commit v1 on v0

--- a/solution.py
+++ b/solution.py
@@ -1,7 +1,14 @@
+import functools
+import math
+
 import jax
 import jax.numpy as jnp
 from jax import lax
+from jax.experimental import pallas as pl
+from jax.experimental.pallas import tpu as pltpu
 from jax.sharding import PartitionSpec as P
+
+MESH = pl.DeviceIdType.MESH
 
 H = 16
 G = 4
@@ -121,9 +128,295 @@
     return (attended, log_mass, owned_cache)
 
 
+PRE, KEY, VAL = range(3)
+NEG = -1e30
+
+
+def fused_kernel(
+    A, B, q_hbm, k_ref, v_ref, pk_ref, pv_ref, len_ref, own_ref, out_ref, log_ref, cache_ref,
+    q_buf, p_buf, k_buf, v_buf, qt, diff, top, total, accum, row_of, q_sem, send, recv,
+):
+    n = A * B * 2
+    tokens, width = k_ref.shape
+    prefix = pk_ref.shape[0]
+    per_group = H // G
+    lanes = per_group * tokens
+    rows = 2 * tokens
+    scale = DH ** (-0.5) * math.log2(math.e)
+    group, me = lax.axis_index("groups"), lax.axis_index("ctx")
+    c = me % 2
+    b = (me // 2) % B
+    a = me // (2 * B)
+    up, down = me + 2 * B, me - 2 * B
+    side, twin = me + 2 * (1 - 2 * b), me + 1 - 2 * c
+    bufs = (p_buf, k_buf, v_buf)
+
+    def shard(a_, b_, c_):
+        return (a_ * B + b_) * 2 + c_
+
+    def move(piece, slot, dest, sem):
+        return pltpu.make_async_remote_copy(
+            src_ref=bufs[piece].at[slot], dst_ref=bufs[piece].at[slot], send_sem=send.at[sem, slot, piece],
+            recv_sem=recv.at[slot, piece], device_id=(group, dest), device_id_type=MESH,
+        )
+
+    def arrived(piece, slot):
+        move(piece, slot, twin, 0).wait_recv()
+
+    q_copy = pltpu.make_async_copy(q_hbm, q_buf, q_sem)
+    q_copy.start()
+
+    barrier = pltpu.get_barrier_semaphore()
+    for dest in (side, twin):
+        pl.semaphore_signal(barrier, inc=1, device_id=(group, dest), device_id_type=MESH)
+
+    @pl.when(a < A - 1)
+    def _():
+        pl.semaphore_signal(barrier, inc=1, device_id=(group, up), device_id_type=MESH)
+
+    @pl.when(a > 0)
+    def _():
+        pl.semaphore_signal(barrier, inc=1, device_id=(group, down), device_id_type=MESH)
+
+    slot_id = lax.broadcasted_iota(jnp.int32, (prefix, DH), 0)
+    lane = lax.broadcasted_iota(jnp.int32, (prefix, DH), 1)
+    owner_row = jnp.full((prefix, DH), -1, jnp.int32)
+    for j in range(own_ref.shape[0]):
+        owner_row = jnp.where(lane // BLK == j, own_ref[j], owner_row)
+    p_buf[me, :, 0:width] = pk_ref[...]
+    p_buf[me, :, width : 2 * width] = pv_ref[...]
+    live = jnp.where(slot_id < len_ref[0], 1.0, 0.0)
+    p_buf[me, :, 2 * width : 2 * width + DH] = live.astype(jnp.bfloat16)
+    p_buf[me, :, 2 * width + DH :] = owner_row.astype(jnp.float32).astype(jnp.bfloat16)
+    k_buf[me] = k_ref[...]
+    v_buf[me] = v_ref[...]
+
+    pl.semaphore_wait(barrier, 2 + jnp.where(a < A - 1, 1, 0) + jnp.where(a > 0, 1, 0))
+
+    def from_below(piece, slot):
+        @pl.when(a < A - 1)
+        def _():
+            move(piece, slot, up, 0).start()
+
+        move(piece, slot, side, 2).start()
+        move(piece, slot, twin, 3).start()
+
+    def from_above(piece, slot):
+        @pl.when(a > 0)
+        def _():
+            move(piece, slot, down, 1).start()
+
+        move(piece, slot, side, 2).start()
+        move(piece, slot, twin, 3).start()
+
+    for piece in (PRE, KEY, VAL):
+        from_below(piece, me)
+
+        @pl.when(a > 0)
+        def _():
+            move(piece, me, down, 1).start()
+
+    q_copy.wait()
+    for g in range(G):
+        heads = [q_buf[:, (g * per_group + j) * DH : (g * per_group + j + 1) * DH] for j in range(per_group)]
+        qt[g] = jnp.concatenate(heads, 0).T
+    diff[...] = lax.broadcasted_iota(jnp.int32, (rows, lanes), 0) - lax.broadcasted_iota(jnp.int32, (rows, lanes), 1) % tokens
+    top[...] = jnp.full(top.shape, NEG, jnp.float32)
+    total[...] = jnp.zeros(total.shape, jnp.float32)
+    accum[...] = jnp.zeros(accum.shape, jnp.float32)
+
+    def fold(g, keys, values, visible):
+        s = jnp.dot(keys, qt[g], preferred_element_type=jnp.float32) * scale
+        s = jnp.where(visible, s, NEG)
+        old = top[g : g + 1]
+        new = jnp.maximum(old, jnp.max(s, axis=0, keepdims=True))
+        w = jnp.exp2(s - new)
+        factor = jnp.exp2(old - new)
+        top[g : g + 1] = new
+        total[g : g + 1] = total[g : g + 1] * factor + jnp.sum(w, axis=0, keepdims=True)
+        mixed = lax.dot_general(
+            values, w.astype(jnp.bfloat16), (((0,), (0,)), ((), ())), preferred_element_type=jnp.float32
+        )
+        accum[g] = accum[g] * factor + mixed
+
+    def attend(unit):
+        limit = me * tokens - unit * rows
+        for g in range(G):
+            at = slice(g * DH, (g + 1) * DH)
+            keys = k_buf[pl.ds(2 * unit, 2), :, at].reshape(rows, DH)
+            values = v_buf[pl.ds(2 * unit, 2), :, at].reshape(rows, DH)
+            fold(g, keys, values, diff[...] <= limit)
+
+    def relay(piece, slot):
+        arrived(piece, slot)
+        move(piece, slot, twin, 3).start()
+
+    relay(PRE, shard(a, 1 - b, c))
+
+    def stage(e, carry):
+        d = e + 1
+
+        @pl.when(a >= e)
+        def _():
+            for piece in (KEY, VAL):
+                arrived(piece, shard(a - e, b, 1 - c))
+            attend((a - e) * B + b)
+
+        for piece in (PRE, KEY, VAL):
+            @pl.when(a >= d)
+            def _():
+                arrived(piece, shard(a - d, b, c))
+                from_below(piece, shard(a - d, b, c))
+
+            @pl.when(a + d < A)
+            def _():
+                arrived(piece, shard(a + d, b, c))
+                from_above(piece, shard(a + d, b, c))
+
+        @pl.when(a >= d)
+        def _():
+            relay(PRE, shard(a - d, 1 - b, c))
+
+        @pl.when(a + d < A)
+        def _():
+            relay(PRE, shard(a + d, 1 - b, c))
+
+        for piece in (KEY, VAL):
+            @pl.when(a >= e)
+            def _():
+                relay(piece, shard(a - e, 1 - b, c))
+
+            @pl.when((a + e < A) & (e > 0))
+            def _():
+                relay(piece, shard(a + e, 1 - b, c))
+
+        @pl.when(a >= e)
+        def _():
+            for piece in (KEY, VAL):
+                arrived(piece, shard(a - e, 1 - b, 1 - c))
+
+        @pl.when((a >= e) & ((e > 0) | (b > 0)))
+        def _():
+            attend((a - e) * B + 1 - b)
+
+        @pl.when(e == A - 2)
+        def _():
+            attend_prefix()
+
+        return carry
+
+    def attend_prefix():
+        for a_ in range(A):
+            for b_ in range(B):
+                arrived(PRE, shard(a_, b_, 1 - c))
+        count = n * prefix
+        whole = lambda lo, hi: p_buf[:, :, lo:hi].reshape(count, hi - lo)
+        alive = whole(2 * width, 2 * width + DH).astype(jnp.float32)
+        alive = jnp.concatenate([alive] * (lanes // DH), 1) > 0.5
+        for g in range(G):
+            lo = g * DH
+            fold(g, whole(lo, lo + DH), whole(width + lo, width + lo + DH), alive)
+        owner = whole(2 * width + DH, 2 * width + 2 * DH).astype(jnp.float32)
+        mine = owner == me.astype(jnp.float32)
+        flag = jnp.where(mine, 1.0, 0.0).astype(jnp.bfloat16)
+        share = 1.0 / BLK
+        from_, to = (lax.broadcasted_iota(jnp.int32, (DH, DH), i) // BLK for i in range(2))
+        before = jnp.where(from_ < to, share, 0.0).astype(jnp.bfloat16)
+        at, other = (lax.broadcasted_iota(jnp.int32, (count, count), i) // prefix for i in range(2))
+        earlier = jnp.where(other < at, 1.0 / prefix, 0.0).astype(jnp.bfloat16)
+        inside = jnp.dot(flag, before, preferred_element_type=jnp.float32)
+        past = jnp.dot(earlier, flag, preferred_element_type=jnp.float32).astype(jnp.bfloat16)
+        past = jnp.dot(past, jnp.full((DH, DH), share, jnp.bfloat16), preferred_element_type=jnp.float32)
+        lane_ = lax.broadcasted_iota(jnp.int32, (count, DH), 1)
+        place = (inside + past) * BLK + (lane_ % BLK).astype(jnp.float32)
+        place = jnp.where(mine, place, -1.0)
+        row_of[...] = jnp.concatenate([place[j * prefix : j * prefix + 8, :tokens] for j in range(n)], 1)
+
+    lax.fori_loop(0, A, stage, 0)
+
+    for g in range(G):
+        result = (accum[g] / total[g : g + 1]).T
+        mass = top[g : g + 1] * math.log(2) + jnp.log(total[g : g + 1])
+        for j in range(per_group):
+            h = g * per_group + j
+            out_ref[:, h * DH : (h + 1) * DH] = result[j * tokens : (j + 1) * tokens].astype(jnp.bfloat16)
+            log_ref[h : h + 1] = mass[:, j * tokens : (j + 1) * tokens]
+
+    for a_ in range(A):
+        for b_ in range(B):
+            @pl.when((a_ > a) )
+            def _():
+                for piece in (KEY, VAL):
+                    arrived(piece, shard(a_, b_, 1 - c))
+
+    slots = cache_ref.shape[0] * BLK
+    hot = lax.broadcasted_iota(jnp.int32, (slots, n * tokens), 0).astype(jnp.float32) == row_of[0:1]
+    hot = jnp.where(hot, 1.0, 0.0).astype(jnp.bfloat16)
+    for at, buf in ((0, k_buf), (width, v_buf)):
+        rows_ = buf[...].reshape(n * tokens, width)
+        picked = jnp.dot(hot, rows_, preferred_element_type=jnp.float32).astype(jnp.bfloat16)
+        cache_ref[:, :, at : at + width] = picked.reshape(slots // BLK, BLK, width)
+
+    for piece in (PRE, KEY, VAL):
+        for a_ in range(A):
+            slot = shard(a_, b, c)
+
+            @pl.when((a_ <= a) & (a < A - 1))
+            def _():
+                move(piece, slot, up, 0).wait_send()
+
+            @pl.when((a_ >= a) & (a > 0))
+            def _():
+                move(piece, slot, down, 1).wait_send()
+
+            move(piece, slot, side, 2).wait_send()
+            move(piece, slot, twin, 3).wait_send()
+            move(piece, shard(a_, 1 - b, c), twin, 3).wait_send()
+
+
+def fused(A, B, queries, new_keys, new_values, prefix_keys, prefix_values, prefix_len, owners):
+    n = A * B * 2
+    tokens, width = new_keys.shape
+    prefix = prefix_keys.shape[0]
+    lanes = H // G * tokens
+    bf16, f32 = jnp.bfloat16, jnp.float32
+    vmem, smem = pl.BlockSpec(memory_space=pltpu.VMEM), pl.BlockSpec(memory_space=pltpu.SMEM)
+    return pl.pallas_call(
+        functools.partial(fused_kernel, A, B),
+        out_shape=(
+            jax.ShapeDtypeStruct((tokens, H * DH), bf16),
+            jax.ShapeDtypeStruct((H, tokens), f32),
+            jax.ShapeDtypeStruct((CAP, BLK, 2 * width), bf16),
+        ),
+        in_specs=[pl.BlockSpec(memory_space=pl.ANY), vmem, vmem, vmem, vmem, smem, smem],
+        out_specs=(vmem, vmem, vmem),
+        scratch_shapes=[
+            pltpu.VMEM((tokens, H * DH), bf16),
+            pltpu.VMEM((n, prefix, 2 * width + 2 * DH), bf16),
+            pltpu.VMEM((n, tokens, width), bf16),
+            pltpu.VMEM((n, tokens, width), bf16),
+            pltpu.VMEM((G, DH, lanes), bf16),
+            pltpu.VMEM((2 * tokens, lanes), jnp.int32),
+            pltpu.VMEM((8, lanes), f32),
+            pltpu.VMEM((8, lanes), f32),
+            pltpu.VMEM((G, DH, lanes), f32),
+            pltpu.VMEM((8, n * tokens), f32),
+            pltpu.SemaphoreType.DMA,
+            pltpu.SemaphoreType.DMA((4, n, 3)),
+            pltpu.SemaphoreType.DMA((n, 3)),
+        ],
+        compiler_params=pltpu.CompilerParams(
+            collective_id=0, has_side_effects=True, vmem_limit_bytes=40 * 1024 * 1024
+        ),
+    )(queries, new_keys, new_values, prefix_keys, prefix_values, prefix_len, owners)
+
+
 def solution(mesh):
+    A = 4
+    B = mesh.shape["ctx"] // (2 * A)
+    body = functools.partial(fused, A, B) if B == 2 else per_device
     return jax.shard_map(
-        per_device,
+        body,
         mesh=mesh,
         in_specs=(
             P(("groups", "ctx"), None),

time: 135 us -> 43.4 us (0.32)
  the two profiles are of different devices: /device:TPU:0 before, /device:TPU:26 now
where the time goes in v1:
time: 43.4 us; the launch traced here: 43.1 us
  Pallas kernels  35.5 us (82%)
  local copies, waits for them, and re-layouts  6.3 us (15%)
  between operations  1.33 us (3%)
    pallas_call x1, Pallas kernels, fused(): pl.pallas_call(functools.partial(fused_kernel, A, B), out_shape=(jax.Shap...  35.5 us
    unnamed x15, local copies, waits for them, and re-layouts  6.3 us

profile of v1, /device:TPU:26, one launch (start us, length us, event | category | flops | bytes accessed | tf_op | source)
XLA Modules:
  0.0 43.1 jit_solution(16966607437536167898)
XLA Ops:
  0.6 0.0 copy-start.5
  1.3 0.0 copy-done.5
  1.3 0.0 copy-start
  1.3 1.0 %copy-done = bf16[96,2048]{1,0:T(8,128)(2,1)S(1)} copy-done((bf16[96,2048]{1,0:T(8,128)(2,1)S(1)}, bf16[96,2048]{1,0:T(8,128)(2,1)}, u32[]{:S(2)}) %copy-start) | copy-done | bytes 393240
  2.3 0.0 copy-start.1
  2.3 0.9 %copy-done.1 = bf16[96,512]{1,0:T(8,128)(2,1)S(1)} copy-done((bf16[96,512]{1,0:T(8,128)(2,1)S(1)}, bf16[96,512]{1,0:T(8,128)(2,1)}, u32[]{:S(2)}) %copy-start.1) | copy-done | bytes 98328
  3.2 0.0 copy-start.2
  3.2 0.9 %copy-done.2 = bf16[96,512]{1,0:T(8,128)(2,1)S(1)} copy-done((bf16[96,512]{1,0:T(8,128)(2,1)S(1)}, bf16[96,512]{1,0:T(8,128)(2,1)}, u32[]{:S(2)}) %copy-start.2) | copy-done | bytes 98328
  4.1 0.0 copy-start.3
  4.1 0.7 %copy-done.3 = bf16[16,512]{1,0:T(8,128)(2,1)S(1)} copy-done((bf16[16,512]{1,0:T(8,128)(2,1)S(1)}, bf16[16,512]{1,0:T(8,128)(2,1)}, u32[]{:S(2)}) %copy-start.3) | copy-done | bytes 16408
  4.8 0.0 copy-start.4
  4.8 0.7 %copy-done.4 = bf16[16,512]{1,0:T(8,128)(2,1)S(1)} copy-done((bf16[16,512]{1,0:T(8,128)(2,1)S(1)}, bf16[16,512]{1,0:T(8,128)(2,1)}, u32[]{:S(2)}) %copy-start.4) | copy-done | bytes 16408
  5.5 35.5 %shard_map.94 = (bf16[96,2048]{1,0:T(8,128)(2,1)S(1)}, f32[16,96]{1,0:T(8,128)S(1)}, bf16[12,16,1024]{2,1,0:T(8,128)(2,1)S(1)}) custom-call(bf16[96,2048]{1,0:T(8,128)(2,1)S(1)} %copy-done, bf16[96,512]{1,0:T(8,128)(2,1)S(1)} %copy-done.1, bf16[96,512]{1,0:T(8,128)(2,1)S(1)} %copy-done.2, bf16[16,512]{1,0:T(8,128)(2,1)S(1)} %copy-done.3, ...), custom_call_target="tpu_custom_call" | custom-call | tf_op jit(solution)/shard_map/pallas_call | solution.py:384
  41.0 0.7 %copy.14 = bf16[96,2048]{1,0:T(8,128)(2,1)} copy(bf16[96,2048]{1,0:T(8,128)(2,1)S(1)} %get-tuple-element.6) | data formatting | bytes 786432
  41.8 0.6 %copy.15 = f32[16,96]{1,0:T(8,128)} copy(f32[16,96]{1,0:T(8,128)S(1)} %get-tuple-element.7) | data formatting | bytes 12288
  42.4 0.7 %copy.16 = bf16[12,16,1024]{2,1,0:T(8,128)(2,1)} copy(bf16[12,16,1024]{2,1,0:T(8,128)(2,1)S(1)} %get-tuple-element.8) | data formatting | bytes 786432
Async XLA Ops:
  0.6 0.7 %copy-start.5 = (s32[6]{0:T(128)S(1)}, s32[6]{0:T(128)}, u32[]{:S(2)}) copy-start(s32[6]{0:T(128)} %own_ref.1) | copy-start | bytes 76
  1.3 1.0 %copy-start = (bf16[96,2048]{1,0:T(8,128)(2,1)S(1)}, bf16[96,2048]{1,0:T(8,128)(2,1)}, u32[]{:S(2)}) copy-start(bf16[96,2048]{1,0:T(8,128)(2,1)} %q_hbm.1) | copy-start | bytes 1179652
  2.3 0.9 %copy-start.1 = (bf16[96,512]{1,0:T(8,128)(2,1)S(1)}, bf16[96,512]{1,0:T(8,128)(2,1)}, u32[]{:S(2)}) copy-start(bf16[96,512]{1,0:T(8,128)(2,1)} %k_ref.1) | copy-start | bytes 294916
  3.2 0.9 %copy-start.2 = (bf16[96,512]{1,0:T(8,128)(2,1)S(1)}, bf16[96,512]{1,0:T(8,128)(2,1)}, u32[]{:S(2)}) copy-start(bf16[96,512]{1,0:T(8,128)(2,1)} %v_ref.1) | copy-start | bytes 294916
  4.1 0.7 %copy-start.3 = (bf16[16,512]{1,0:T(8,128)(2,1)S(1)}, bf16[16,512]{1,0:T(8,128)(2,1)}, u32[]{:S(2)}) copy-start(bf16[16,512]{1,0:T(8,128)(2,1)} %pk_ref.1) | copy-start | bytes 49156
  4.8 0.7 %copy-start.4 = (bf16[16,512]{1,0:T(8,128)(2,1)S(1)}, bf16[16,512]{1,0:T(8,128)(2,1)}, u32[]{:S(2)}) copy-start(bf16[16,512]{1,0:T(8,128)(2,1)} %pv_ref.1) | copy-start | bytes 49156

commit v2 on v1

--- a/solution.py
+++ b/solution.py
@@ -130,11 +130,12 @@
 
 PRE, KEY, VAL = range(3)
 NEG = -1e30
+VMEM_BYTES = 40 * 1024 * 1024
 
 
 def fused_kernel(
-    A, B, q_hbm, k_ref, v_ref, pk_ref, pv_ref, len_ref, own_ref, out_ref, log_ref, cache_ref,
-    q_buf, p_buf, k_buf, v_buf, qt, diff, top, total, accum, row_of, q_sem, send, recv,
+    A, B, q_hbm, k_ref, v_ref, pk_ref, pv_ref, len_hbm, own_hbm, out_ref, log_ref, cache_ref,
+    q_buf, p_buf, k_buf, v_buf, len_ref, own_ref, qt, diff, top, total, accum, row_of, load, send, recv,
 ):
     n = A * B * 2
     tokens, width = k_ref.shape
@@ -163,8 +164,16 @@
     def arrived(piece, slot):
         move(piece, slot, twin, 0).wait_recv()
 
-    q_copy = pltpu.make_async_copy(q_hbm, q_buf, q_sem)
-    q_copy.start()
+    loads = [
+        pltpu.make_async_copy(src, dst, load.at[i])
+        for i, (src, dst) in enumerate((
+            (own_hbm, own_ref), (len_hbm, len_ref),
+            (k_ref, k_buf.at[me]), (v_ref, v_buf.at[me]),
+            (pk_ref, p_buf.at[me, :, 0:width]), (pv_ref, p_buf.at[me, :, width : 2 * width]), (q_hbm, q_buf),
+        ))
+    ]
+    for copy in loads:
+        copy.start()
 
     barrier = pltpu.get_barrier_semaphore()
     for dest in (side, twin):
@@ -180,16 +189,14 @@
 
     slot_id = lax.broadcasted_iota(jnp.int32, (prefix, DH), 0)
     lane = lax.broadcasted_iota(jnp.int32, (prefix, DH), 1)
+    loads[0].wait()
+    loads[1].wait()
     owner_row = jnp.full((prefix, DH), -1, jnp.int32)
     for j in range(own_ref.shape[0]):
         owner_row = jnp.where(lane // BLK == j, own_ref[j], owner_row)
-    p_buf[me, :, 0:width] = pk_ref[...]
-    p_buf[me, :, width : 2 * width] = pv_ref[...]
     live = jnp.where(slot_id < len_ref[0], 1.0, 0.0)
     p_buf[me, :, 2 * width : 2 * width + DH] = live.astype(jnp.bfloat16)
     p_buf[me, :, 2 * width + DH :] = owner_row.astype(jnp.float32).astype(jnp.bfloat16)
-    k_buf[me] = k_ref[...]
-    v_buf[me] = v_ref[...]
 
     pl.semaphore_wait(barrier, 2 + jnp.where(a < A - 1, 1, 0) + jnp.where(a > 0, 1, 0))
 
@@ -209,14 +216,16 @@
         move(piece, slot, side, 2).start()
         move(piece, slot, twin, 3).start()
 
-    for piece in (PRE, KEY, VAL):
+    for piece, needs in ((KEY, loads[2:3]), (PRE, loads[4:6]), (VAL, loads[3:4])):
+        for copy in needs:
+            copy.wait()
         from_below(piece, me)
 
         @pl.when(a > 0)
         def _():
             move(piece, me, down, 1).start()
 
-    q_copy.wait()
+    loads[6].wait()
     for g in range(G):
         heads = [q_buf[:, (g * per_group + j) * DH : (g * per_group + j + 1) * DH] for j in range(per_group)]
         qt[g] = jnp.concatenate(heads, 0).T
@@ -344,7 +353,7 @@
 
     for a_ in range(A):
         for b_ in range(B):
-            @pl.when((a_ > a) )
+            @pl.when(a_ > a)
             def _():
                 for piece in (KEY, VAL):
                     arrived(piece, shard(a_, b_, 1 - c))
@@ -374,41 +383,59 @@
             move(piece, shard(a_, 1 - b, c), twin, 3).wait_send()
 
 
+def write_results(*refs):
+    copies = [pltpu.make_async_copy(refs[i], refs[3 + i], refs[6].at[i]) for i in range(3)]
+    for copy in copies:
+        copy.start()
+    for copy in copies:
+        copy.wait()
+
+
 def fused(A, B, queries, new_keys, new_values, prefix_keys, prefix_values, prefix_len, owners):
     n = A * B * 2
     tokens, width = new_keys.shape
     prefix = prefix_keys.shape[0]
     lanes = H // G * tokens
     bf16, f32 = jnp.bfloat16, jnp.float32
-    vmem, smem = pl.BlockSpec(memory_space=pltpu.VMEM), pl.BlockSpec(memory_space=pltpu.SMEM)
-    return pl.pallas_call(
+    vmem, hbm = pl.BlockSpec(memory_space=pltpu.VMEM), pl.BlockSpec(memory_space=pltpu.HBM)
+    arrays = (queries, new_keys, new_values, prefix_keys, prefix_values)
+    results = pl.pallas_call(
         functools.partial(fused_kernel, A, B),
         out_shape=(
             jax.ShapeDtypeStruct((tokens, H * DH), bf16),
             jax.ShapeDtypeStruct((H, tokens), f32),
             jax.ShapeDtypeStruct((CAP, BLK, 2 * width), bf16),
         ),
-        in_specs=[pl.BlockSpec(memory_space=pl.ANY), vmem, vmem, vmem, vmem, smem, smem],
-        out_specs=(vmem, vmem, vmem),
+        in_specs=[hbm] * 7,
+        out_specs=(vmem,) * 3,
         scratch_shapes=[
             pltpu.VMEM((tokens, H * DH), bf16),
             pltpu.VMEM((n, prefix, 2 * width + 2 * DH), bf16),
             pltpu.VMEM((n, tokens, width), bf16),
             pltpu.VMEM((n, tokens, width), bf16),
+            pltpu.SMEM(prefix_len.shape, jnp.int32),
+            pltpu.SMEM(owners.shape, jnp.int32),
             pltpu.VMEM((G, DH, lanes), bf16),
             pltpu.VMEM((2 * tokens, lanes), jnp.int32),
             pltpu.VMEM((8, lanes), f32),
             pltpu.VMEM((8, lanes), f32),
             pltpu.VMEM((G, DH, lanes), f32),
             pltpu.VMEM((8, n * tokens), f32),
-            pltpu.SemaphoreType.DMA,
+            pltpu.SemaphoreType.DMA((7,)),
             pltpu.SemaphoreType.DMA((4, n, 3)),
             pltpu.SemaphoreType.DMA((n, 3)),
         ],
         compiler_params=pltpu.CompilerParams(
-            collective_id=0, has_side_effects=True, vmem_limit_bytes=40 * 1024 * 1024
+            collective_id=0, has_side_effects=True, vmem_limit_bytes=VMEM_BYTES
         ),
-    )(queries, new_keys, new_values, prefix_keys, prefix_values, prefix_len, owners)
+    )(*(pltpu.with_memory_space_constraint(x, pltpu.HBM) for x in arrays), prefix_len, pltpu.with_memory_space_constraint(owners, pltpu.HBM))
+    return pl.pallas_call(
+        write_results,
+        out_shape=tuple(jax.ShapeDtypeStruct(x.shape, x.dtype) for x in results),
+        in_specs=[vmem] * 3,
+        out_specs=(hbm,) * 3,
+        scratch_shapes=[pltpu.SemaphoreType.DMA((3,))],
+    )(*results)
 
 
 def solution(mesh):

time: 43.4 us -> 41.8 us (0.963)
  local copies, waits for them, and re-layouts: 6.3 us -> 2.08 us
  Pallas kernels: 35.5 us -> 38.3 us
    unnamed x15 -> x6, local copies, waits for them, and re-layouts: 6.3 us -> 2.08 us
    pallas_call x0 -> x1, Pallas kernels: none -> 2.03 us  [fused(): pl.pallas_call(write_results, out_shape=tuple((jax.ShapeDtypeStruct(x.sha...]
    pallas_call x1, Pallas kernels: 35.5 us -> 36.2 us  [fused(): pl.pallas_call(functools.partial(fused_kernel, A, B), out_shape=(jax.Shap...]
where the time goes in v2:
time: 41.8 us; the launch traced here: 41.7 us
  Pallas kernels  38.3 us (92%)
  local copies, waits for them, and re-layouts  2.08 us (5%)
  between operations  1.3 us (3%)
    pallas_call x1, Pallas kernels, fused(): pl.pallas_call(functools.partial(fused_kernel, A, B), out_shape=(jax.Shap...  36.2 us
    unnamed x6, local copies, waits for them, and re-layouts  2.08 us
    pallas_call x1, Pallas kernels, fused(): pl.pallas_call(write_results, out_shape=tuple((jax.ShapeDtypeStruct(x.sha...  2.03 us

profile of v2, /device:TPU:26, one launch (start us, length us, event | category | flops | bytes accessed | tf_op | source)
XLA Modules:
  0.0 41.7 jit_solution(8446097617602610491)
XLA Ops:
  1.3 36.2 %shard_map.94 = (bf16[96,2048]{1,0:T(8,128)(2,1)S(1)}, f32[16,96]{1,0:T(8,128)S(1)}, bf16[12,16,1024]{2,1,0:T(8,128)(2,1)S(1)}) custom-call(bf16[96,2048]{1,0:T(8,128)(2,1)} %q_hbm.1, bf16[96,512]{1,0:T(8,128)(2,1)} %k_ref.1, bf16[96,512]{1,0:T(8,128)(2,1)} %v_ref.1, bf16[16,512]{1,0:T(8,128)(2,1)} %pk_ref.1, bf16[16,512]{1,0:T(8,128)(2,1)} %pv_ref.1, ...), custom_call_target="tpu_custom_call" | custom-call | tf_op jit(solution)/shard_map/pallas_call | solution.py:402
  37.5 0.0 copy-start
  37.5 0.7 %copy-done = bf16[96,2048]{1,0:T(8,128)(2,1)} copy-done((bf16[96,2048]{1,0:T(8,128)(2,1)}, bf16[96,2048]{1,0:T(8,128)(2,1)S(1)}, u32[]{:S(2)}) %copy-start) | copy-done | bytes 393240
  38.3 0.0 copy-start.1
  38.3 0.7 %copy-done.1 = bf16[12,16,1024]{2,1,0:T(8,128)(2,1)} copy-done((bf16[12,16,1024]{2,1,0:T(8,128)(2,1)}, bf16[12,16,1024]{2,1,0:T(8,128)(2,1)S(1)}, u32[]{:S(2)}) %copy-start.1) | copy-done | bytes 393240
  39.0 0.0 copy-start.2
  39.0 0.6 %copy-done.2 = f32[16,96]{1,0:T(8,128)} copy-done((f32[16,96]{1,0:T(8,128)}, f32[16,96]{1,0:T(8,128)S(1)}, u32[]{:S(2)}) %copy-start.2) | copy-done | bytes 6168
  39.6 2.0 %shard_map.95 = (bf16[96,2048]{1,0:T(8,128)(2,1)}, f32[16,96]{1,0:T(8,128)}, bf16[12,16,1024]{2,1,0:T(8,128)(2,1)}) custom-call(bf16[96,2048]{1,0:T(8,128)(2,1)} %copy-done, f32[16,96]{1,0:T(8,128)} %copy-done.2, bf16[12,16,1024]{2,1,0:T(8,128)(2,1)} %copy-done.1), custom_call_target="tpu_custom_call" | custom-call | tf_op jit(solution)/shard_map/pallas_call | solution.py:432
Async XLA Ops:
  37.5 0.8 %copy-start = (bf16[96,2048]{1,0:T(8,128)(2,1)}, bf16[96,2048]{1,0:T(8,128)(2,1)S(1)}, u32[]{:S(2)}) copy-start(bf16[96,2048]{1,0:T(8,128)(2,1)S(1)} %get-tuple-element.6.refs_0_) | copy-start | bytes 1179652
  38.3 0.7 %copy-start.1 = (bf16[12,16,1024]{2,1,0:T(8,128)(2,1)}, bf16[12,16,1024]{2,1,0:T(8,128)(2,1)S(1)}, u32[]{:S(2)}) copy-start(bf16[12,16,1024]{2,1,0:T(8,128)(2,1)S(1)} %get-tuple-element.8.refs_2_) | copy-start | bytes 1179652
  39.0 0.6 %copy-start.2 = (f32[16,96]{1,0:T(8,128)}, f32[16,96]{1,0:T(8,128)S(1)}, u32[]{:S(2)}) copy-start(f32[16,96]{1,0:T(8,128)S(1)} %get-tuple-element.7.refs_1_) | copy-start | bytes 18436

commit v3 on v2

--- a/solution.py
+++ b/solution.py
@@ -194,9 +194,9 @@
     owner_row = jnp.full((prefix, DH), -1, jnp.int32)
     for j in range(own_ref.shape[0]):
         owner_row = jnp.where(lane // BLK == j, own_ref[j], owner_row)
-    live = jnp.where(slot_id < len_ref[0], 1.0, 0.0)
-    p_buf[me, :, 2 * width : 2 * width + DH] = live.astype(jnp.bfloat16)
-    p_buf[me, :, 2 * width + DH :] = owner_row.astype(jnp.float32).astype(jnp.bfloat16)
+    meta = jnp.where(lane < tokens, owner_row, jnp.where(slot_id < len_ref[0], 1, 0))
+    p_buf[me, :, 2 * width :] = meta.astype(jnp.float32).astype(jnp.bfloat16)
+    cache_ref[...] = jnp.zeros(cache_ref.shape, cache_ref.dtype)
 
     pl.semaphore_wait(barrier, 2 + jnp.where(a < A - 1, 1, 0) + jnp.where(a > 0, 1, 0))
 
@@ -216,7 +216,7 @@
         move(piece, slot, side, 2).start()
         move(piece, slot, twin, 3).start()
 
-    for piece, needs in ((KEY, loads[2:3]), (PRE, loads[4:6]), (VAL, loads[3:4])):
+    for piece, needs in ((PRE, loads[4:6]), (KEY, loads[2:3]), (VAL, loads[3:4])):
         for copy in needs:
             copy.wait()
         from_below(piece, me)
@@ -236,7 +236,8 @@
 
     def fold(g, keys, values, visible):
         s = jnp.dot(keys, qt[g], preferred_element_type=jnp.float32) * scale
-        s = jnp.where(visible, s, NEG)
+        if visible is not None:
+            s = jnp.where(visible, s, NEG)
         old = top[g : g + 1]
         new = jnp.maximum(old, jnp.max(s, axis=0, keepdims=True))
         w = jnp.exp2(s - new)
@@ -248,56 +249,61 @@
         )
         accum[g] = accum[g] * factor + mixed
 
-    def attend(unit):
-        limit = me * tokens - unit * rows
+    def attend(unit, own=False):
+        limit = (me - 2 * unit) * tokens
         for g in range(G):
             at = slice(g * DH, (g + 1) * DH)
             keys = k_buf[pl.ds(2 * unit, 2), :, at].reshape(rows, DH)
             values = v_buf[pl.ds(2 * unit, 2), :, at].reshape(rows, DH)
-            fold(g, keys, values, diff[...] <= limit)
+            fold(g, keys, values, diff[...] <= limit if own else None)
 
     def relay(piece, slot):
         arrived(piece, slot)
         move(piece, slot, twin, 3).start()
 
-    relay(PRE, shard(a, 1 - b, c))
+    def direct(piece, d):
+        @pl.when(a >= d)
+        def _():
+            arrived(piece, shard(a - d, b, c))
+            from_below(piece, shard(a - d, b, c))
+
+        @pl.when(a + d < A)
+        def _():
+            arrived(piece, shard(a + d, b, c))
+            from_above(piece, shard(a + d, b, c))
+
+    def across(piece, e):
+        @pl.when(a >= e)
+        def _():
+            relay(piece, shard(a - e, 1 - b, c))
+
+        @pl.when((a + e < A) & (e > 0))
+        def _():
+            relay(piece, shard(a + e, 1 - b, c))
 
     def stage(e, carry):
-        d = e + 1
-
-        @pl.when(a >= e)
+        @pl.when((a >= e) & (e > 0))
         def _():
             for piece in (KEY, VAL):
                 arrived(piece, shard(a - e, b, 1 - c))
             attend((a - e) * B + b)
 
+        @pl.when(e == A - 1)
+        def _():
+            def near(a_, carry_):
+                @pl.when((a_ - a < A - 1) & (a - a_ < A - 1))
+                def _():
+                    place_slab(a_)
+
+                return carry_
+
+            lax.fori_loop(0, A, near, 0)
+
         for piece in (PRE, KEY, VAL):
-            @pl.when(a >= d)
-            def _():
-                arrived(piece, shard(a - d, b, c))
-                from_below(piece, shard(a - d, b, c))
-
-            @pl.when(a + d < A)
-            def _():
-                arrived(piece, shard(a + d, b, c))
-                from_above(piece, shard(a + d, b, c))
-
-        @pl.when(a >= d)
-        def _():
-            relay(PRE, shard(a - d, 1 - b, c))
-
-        @pl.when(a + d < A)
-        def _():
-            relay(PRE, shard(a + d, 1 - b, c))
-
-        for piece in (KEY, VAL):
-            @pl.when(a >= e)
-            def _():
-                relay(piece, shard(a - e, 1 - b, c))
-
-            @pl.when((a + e < A) & (e > 0))
-            def _():
-                relay(piece, shard(a + e, 1 - b, c))
+            direct(piece, e + 1)
+        across(PRE, e + 1)
+        across(KEY, e)
+        across(VAL, e)
 
         @pl.when(a >= e)
         def _():
@@ -313,6 +319,21 @@
             attend_prefix()
 
         return carry
+
+    def place_slab(a_):
+        @pl.when(a_ > a)
+        def _():
+            for b_ in range(B):
+                for piece in (KEY, VAL):
+                    arrived(piece, shard(a_, b_, 1 - c))
+
+        slots, slab = cache_ref.shape[0] * BLK, 2 * B * tokens
+        hot = lax.broadcasted_iota(jnp.int32, (slots, slab), 0).astype(jnp.float32) == row_of[a_, 0:1]
+        hot = jnp.where(hot, 1.0, 0.0).astype(jnp.bfloat16)
+        for at, buf in ((0, k_buf), (width, v_buf)):
+            rows_ = buf[pl.ds(a_ * 2 * B, 2 * B)].reshape(slab, width)
+            picked = jnp.dot(hot, rows_, preferred_element_type=jnp.float32).astype(jnp.bfloat16)
+            cache_ref[:, :, at : at + width] += picked.reshape(slots // BLK, BLK, width)
 
     def attend_prefix():
         for a_ in range(A):
@@ -320,13 +341,13 @@
                 arrived(PRE, shard(a_, b_, 1 - c))
         count = n * prefix
         whole = lambda lo, hi: p_buf[:, :, lo:hi].reshape(count, hi - lo)
-        alive = whole(2 * width, 2 * width + DH).astype(jnp.float32)
-        alive = jnp.concatenate([alive] * (lanes // DH), 1) > 0.5
+        meta = whole(2 * width, 2 * width + DH).astype(jnp.float32)
+        alive = jnp.broadcast_to(meta[:, tokens : tokens + 1], (count, lanes)) > 0.5
         for g in range(G):
             lo = g * DH
             fold(g, whole(lo, lo + DH), whole(width + lo, width + lo + DH), alive)
-        owner = whole(2 * width + DH, 2 * width + 2 * DH).astype(jnp.float32)
-        mine = owner == me.astype(jnp.float32)
+        lane_ = lax.broadcasted_iota(jnp.int32, (count, DH), 1)
+        mine = (meta == me.astype(jnp.float32)) & (lane_ < tokens)
         flag = jnp.where(mine, 1.0, 0.0).astype(jnp.bfloat16)
         share = 1.0 / BLK
         from_, to = (lax.broadcasted_iota(jnp.int32, (DH, DH), i) // BLK for i in range(2))
@@ -336,11 +357,16 @@
         inside = jnp.dot(flag, before, preferred_element_type=jnp.float32)
         past = jnp.dot(earlier, flag, preferred_element_type=jnp.float32).astype(jnp.bfloat16)
         past = jnp.dot(past, jnp.full((DH, DH), share, jnp.bfloat16), preferred_element_type=jnp.float32)
-        lane_ = lax.broadcasted_iota(jnp.int32, (count, DH), 1)
         place = (inside + past) * BLK + (lane_ % BLK).astype(jnp.float32)
         place = jnp.where(mine, place, -1.0)
-        row_of[...] = jnp.concatenate([place[j * prefix : j * prefix + 8, :tokens] for j in range(n)], 1)
-
+        for a_ in range(A):
+            slab = [place[j * prefix : j * prefix + 8, :tokens] for j in range(2 * B * a_, 2 * B * (a_ + 1))]
+            row_of[a_] = jnp.concatenate(slab, 1)
+
+    for piece in (KEY, VAL):
+        arrived(piece, twin)
+    attend(a * B + b, own=True)
+    across(PRE, 0)
     lax.fori_loop(0, A, stage, 0)
 
     for g in range(G):
@@ -351,20 +377,9 @@
             out_ref[:, h * DH : (h + 1) * DH] = result[j * tokens : (j + 1) * tokens].astype(jnp.bfloat16)
             log_ref[h : h + 1] = mass[:, j * tokens : (j + 1) * tokens]
 
-    for a_ in range(A):
-        for b_ in range(B):
-            @pl.when(a_ > a)
-            def _():
-                for piece in (KEY, VAL):
-                    arrived(piece, shard(a_, b_, 1 - c))
-
-    slots = cache_ref.shape[0] * BLK
-    hot = lax.broadcasted_iota(jnp.int32, (slots, n * tokens), 0).astype(jnp.float32) == row_of[0:1]
-    hot = jnp.where(hot, 1.0, 0.0).astype(jnp.bfloat16)
-    for at, buf in ((0, k_buf), (width, v_buf)):
-        rows_ = buf[...].reshape(n * tokens, width)
-        picked = jnp.dot(hot, rows_, preferred_element_type=jnp.float32).astype(jnp.bfloat16)
-        cache_ref[:, :, at : at + width] = picked.reshape(slots // BLK, BLK, width)
+    @pl.when((a == 0) | (a == A - 1))
+    def _():
+        place_slab(A - 1 - a)
 
     for piece in (PRE, KEY, VAL):
         for a_ in range(A):
@@ -398,6 +413,7 @@
     lanes = H // G * tokens
     bf16, f32 = jnp.bfloat16, jnp.float32
     vmem, hbm = pl.BlockSpec(memory_space=pltpu.VMEM), pl.BlockSpec(memory_space=pltpu.HBM)
+    assert tokens < DH
     arrays = (queries, new_keys, new_values, prefix_keys, prefix_values)
     results = pl.pallas_call(
         functools.partial(fused_kernel, A, B),
@@ -410,7 +426,7 @@
         out_specs=(vmem,) * 3,
         scratch_shapes=[
             pltpu.VMEM((tokens, H * DH), bf16),
-            pltpu.VMEM((n, prefix, 2 * width + 2 * DH), bf16),
+            pltpu.VMEM((n, prefix, 2 * width + DH), bf16),
             pltpu.VMEM((n, tokens, width), bf16),
             pltpu.VMEM((n, tokens, width), bf16),
             pltpu.SMEM(prefix_len.shape, jnp.int32),
@@ -420,7 +436,7 @@
             pltpu.VMEM((8, lanes), f32),
             pltpu.VMEM((8, lanes), f32),
             pltpu.VMEM((G, DH, lanes), f32),
-            pltpu.VMEM((8, n * tokens), f32),
+            pltpu.VMEM((A, 8, 2 * B * tokens), f32),
             pltpu.SemaphoreType.DMA((7,)),
             pltpu.SemaphoreType.DMA((4, n, 3)),
             pltpu.SemaphoreType.DMA((n, 3)),
@@ -435,6 +451,7 @@
         in_specs=[vmem] * 3,
         out_specs=(hbm,) * 3,
         scratch_shapes=[pltpu.SemaphoreType.DMA((3,))],
+        compiler_params=pltpu.CompilerParams(vmem_limit_bytes=4 * 1024 * 1024),
     )(*results)
 
 

time: 41.8 us -> 37.7 us (0.902)
  Pallas kernels: 38.3 us -> 36.2 us
  local copies, waits for them, and re-layouts: 2.08 us -> 0 us
    unnamed x6 -> x0, local copies, waits for them, and re-layouts: 2.08 us -> none
    pallas_call x1, Pallas kernels: 2.03 us -> 0.91 us  [fused(): pl.pallas_call(write_results, out_shape=tuple((jax.ShapeDtypeStruct(x.sha...]
    pallas_call x1, Pallas kernels: 36.2 us -> 35.3 us  [fused(): pl.pallas_call(functools.partial(fused_kernel, A, B), out_shape=(jax.Shap...]
where the time goes in v3:
time: 37.7 us; the launch traced here: 37.5 us
  Pallas kernels  36.2 us (96%)
  between operations  1.29 us (3%)
    pallas_call x1, Pallas kernels, fused(): pl.pallas_call(functools.partial(fused_kernel, A, B), out_shape=(jax.Shap...  35.3 us
    pallas_call x1, Pallas kernels, fused(): pl.pallas_call(write_results, out_shape=tuple((jax.ShapeDtypeStruct(x.sha...  0.91 us

profile of v3, /device:TPU:26, one launch (start us, length us, event | category | flops | bytes accessed | tf_op | source)
XLA Modules:
  0.0 37.5 jit_solution(16348523895823515864)
XLA Ops:
  1.3 35.3 %shard_map.94 = (bf16[96,2048]{1,0:T(8,128)(2,1)S(1)}, f32[16,96]{1,0:T(8,128)S(1)}, bf16[12,16,1024]{2,1,0:T(8,128)(2,1)S(1)}) custom-call(bf16[96,2048]{1,0:T(8,128)(2,1)} %q_hbm.1, bf16[96,512]{1,0:T(8,128)(2,1)} %k_ref.1, bf16[96,512]{1,0:T(8,128)(2,1)} %v_ref.1, bf16[16,512]{1,0:T(8,128)(2,1)} %pk_ref.1, bf16[16,512]{1,0:T(8,128)(2,1)} %pv_ref.1, ...), custom_call_target="tpu_custom_call" | custom-call | tf_op jit(solution)/shard_map/pallas_call | solution.py:418
  36.6 0.9 %shard_map.95 = (bf16[96,2048]{1,0:T(8,128)(2,1)}, f32[16,96]{1,0:T(8,128)}, bf16[12,16,1024]{2,1,0:T(8,128)(2,1)}) custom-call(bf16[96,2048]{1,0:T(8,128)(2,1)S(1)} %get-tuple-element.6.refs_0_, f32[16,96]{1,0:T(8,128)S(1)} %get-tuple-element.7.refs_1_, bf16[12,16,1024]{2,1,0:T(8,128)(2,1)S(1)} %get-tuple-element.8.refs_2_), custom_call_target="tpu_custom_call" | custom-call | tf_op jit(solution)/shard_map/pallas_call | solution.py:448

commit v4 on v3

--- a/solution.py
+++ b/solution.py
@@ -200,20 +200,28 @@
 
     pl.semaphore_wait(barrier, 2 + jnp.where(a < A - 1, 1, 0) + jnp.where(a > 0, 1, 0))
 
-    def from_below(piece, slot):
+    def to_side(piece, slot, d):
+        if piece == KEY:
+            @pl.when(d < A - 1)
+            def _():
+                move(piece, slot, side, 2).start()
+        else:
+            move(piece, slot, side, 2).start()
+
+    def from_below(piece, slot, d=0):
         @pl.when(a < A - 1)
         def _():
             move(piece, slot, up, 0).start()
 
-        move(piece, slot, side, 2).start()
+        to_side(piece, slot, d)
         move(piece, slot, twin, 3).start()
 
-    def from_above(piece, slot):
+    def from_above(piece, slot, d=0):
         @pl.when(a > 0)
         def _():
             move(piece, slot, down, 1).start()
 
-        move(piece, slot, side, 2).start()
+        to_side(piece, slot, d)
         move(piece, slot, twin, 3).start()
 
     for piece, needs in ((PRE, loads[4:6]), (KEY, loads[2:3]), (VAL, loads[3:4])):
@@ -265,21 +273,31 @@
         @pl.when(a >= d)
         def _():
             arrived(piece, shard(a - d, b, c))
-            from_below(piece, shard(a - d, b, c))
+            from_below(piece, shard(a - d, b, c), d)
 
         @pl.when(a + d < A)
         def _():
             arrived(piece, shard(a + d, b, c))
-            from_above(piece, shard(a + d, b, c))
+            from_above(piece, shard(a + d, b, c), d)
 
     def across(piece, e):
         @pl.when(a >= e)
         def _():
             relay(piece, shard(a - e, 1 - b, c))
 
+            if piece == KEY:
+                @pl.when((e == A - 2) & (a == A - 2))
+                def _():
+                    move(piece, shard(a - e, 1 - b, c), up, 0).start()
+
         @pl.when((a + e < A) & (e > 0))
         def _():
             relay(piece, shard(a + e, 1 - b, c))
+
+            if piece == KEY:
+                @pl.when((e == A - 2) & (a == 1))
+                def _():
+                    move(piece, shard(a + e, 1 - b, c), down, 1).start()
 
     def stage(e, carry):
         @pl.when((a >= e) & (e > 0))
@@ -301,9 +319,9 @@
 
         for piece in (PRE, KEY, VAL):
             direct(piece, e + 1)
-        across(PRE, e + 1)
         across(KEY, e)
         across(VAL, e)
+        across(PRE, e + 1)
 
         @pl.when(a >= e)
         def _():
@@ -393,9 +411,20 @@
             def _():
                 move(piece, slot, down, 1).wait_send()
 
-            move(piece, slot, side, 2).wait_send()
+            @pl.when((piece != KEY) | ((a - a_ < A - 1) & (a_ - a < A - 1)))
+            def _():
+                move(piece, slot, side, 2).wait_send()
+
             move(piece, slot, twin, 3).wait_send()
             move(piece, shard(a_, 1 - b, c), twin, 3).wait_send()
+
+    @pl.when(a == A - 2)
+    def _():
+        move(KEY, shard(0, 1 - b, c), up, 0).wait_send()
+
+    @pl.when(a == 1)
+    def _():
+        move(KEY, shard(A - 1, 1 - b, c), down, 1).wait_send()
 
 
 def write_results(*refs):

time: 37.7 us -> 34.7 us (0.920)
  the two profiles are of different devices: /device:TPU:26 before, /device:TPU:27 now
where the time goes in v4:
time: 34.7 us; the launch traced here: 34.6 us
  Pallas kernels  33.3 us (96%)
  between operations  1.29 us (4%)
    pallas_call x1, Pallas kernels, fused(): pl.pallas_call(functools.partial(fused_kernel, A, B), out_shape=(jax.Shap...  32.4 us
    pallas_call x1, Pallas kernels, fused(): pl.pallas_call(write_results, out_shape=tuple((jax.ShapeDtypeStruct(x.sha...  0.91 us

profile of v4, /device:TPU:27, one launch (start us, length us, event | category | flops | bytes accessed | tf_op | source)
XLA Modules:
  0.0 34.6 jit_solution(10209852466060760608)
XLA Ops:
  1.3 32.4 %shard_map.94 = (bf16[96,2048]{1,0:T(8,128)(2,1)S(1)}, f32[16,96]{1,0:T(8,128)S(1)}, bf16[12,16,1024]{2,1,0:T(8,128)(2,1)S(1)}) custom-call(bf16[96,2048]{1,0:T(8,128)(2,1)} %q_hbm.1, bf16[96,512]{1,0:T(8,128)(2,1)} %k_ref.1, bf16[96,512]{1,0:T(8,128)(2,1)} %v_ref.1, bf16[16,512]{1,0:T(8,128)(2,1)} %pk_ref.1, bf16[16,512]{1,0:T(8,128)(2,1)} %pv_ref.1, ...), custom_call_target="tpu_custom_call" | custom-call | tf_op jit(solution)/shard_map/pallas_call | solution.py:447
  33.7 0.9 %shard_map.95 = (bf16[96,2048]{1,0:T(8,128)(2,1)}, f32[16,96]{1,0:T(8,128)}, bf16[12,16,1024]{2,1,0:T(8,128)(2,1)}) custom-call(bf16[96,2048]{1,0:T(8,128)(2,1)S(1)} %get-tuple-element.6.refs_0_, f32[16,96]{1,0:T(8,128)S(1)} %get-tuple-element.7.refs_1_, bf16[12,16,1024]{2,1,0:T(8,128)(2,1)S(1)} %get-tuple-element.8.refs_2_), custom_call_target="tpu_custom_call" | custom-call | tf_op jit(solution)/shard_map/pallas_call | solution.py:477
